TPU v7x, 512 devices: a whole 4x4x16 slice. The times are simulated.
512 devices in a mesh: pipe: 8 (over x, core), dp: 64 (over y, z).
Axes of the slice: x: 4, y: 4, z: 16, core: 2. Of those that a mesh axis runs over, the one named last changes fastest.
Arguments:
- acts: bfloat16 [8, 8192, 8192], P('pipe', 'dp'), may hold values from -6 to 6
- incoming: bfloat16 [8, 8192, 8192], P('pipe', 'dp'), may hold values from -6 to 6
- proj_in: bfloat16 [64, 8192], P(None, 'dp'), may hold values from -0.0625 to 0.0625
- proj_out: bfloat16 [64, 8192], P(None, 'dp'), may hold values from -0.0625 to 0.0625
- valid_rows: bfloat16 [8, 128, 4096], P('pipe', 'dp'), may hold values from -0.09375 to 0.09375
- lengths: int32 [64], P('dp'), may hold values from 1 to 128, 7168 in all
- domains: int32 [64], replicated, may hold values from 0 to 63
Outputs:
- domain_gram: float32 [8, 64, 128, 128], P('pipe', 'dp')
All inputs are finite; a program needn't handle non-finite values. No bound on the sum of `lengths` on one device may be relied on, other than what follows from the above.
Results may differ from a plain program's by a relative error of at most 0.004.
Values may be sent and summed in bfloat16 or wider, within the bound.
No kernel may reach another device: no remote copies, remote signals or barrier semaphores. Data moves between devices by JAX's collectives and lax.ppermute only.
A program may use at most 128 MiB of HBM per device.

v0:
```python
import jax
import jax.numpy as jnp
from jax import lax
from jax.sharding import PartitionSpec as P

highest_precision = lax.Precision.HIGHEST


def entering(value, axis, combine, identity):
    length, place = (lax.axis_size(axis), lax.axis_index(axis))
    everything = lax.all_gather(value.astype(jnp.bfloat16), axis)
    start = jnp.broadcast_to(jnp.asarray(identity, value.dtype), value.shape)

    def lap(k, before):
        at = length - 1 - k
        reached = at > place
        new = combine(before, everything[at].astype(value.dtype))
        return jnp.where(reached, new, before)

    return lax.fori_loop(0, length, lap, start)


def add_terms(earlier, later):
    return earlier + later


def body(acts, incoming, proj_in, proj_out, valid_rows, lengths, domains):
    layer_act = acts[0]
    branch = incoming[0]
    rows_here = layer_act.shape[0]
    proj_size = proj_in.shape[0]
    grad_term = branch.astype(jnp.float32)
    above = entering(grad_term, "pipe", add_terms, jnp.zeros_like(grad_term))
    source = above + grad_term
    empty = jnp.zeros((rows_here, proj_size), jnp.float32)
    pieces = (
        lax.all_gather(proj_in, "dp", axis=1, tiled=True),
        lax.all_gather(proj_out, "dp", axis=1, tiled=True),
    )
    new_act = lax.dot_general(
        layer_act, pieces[0], (((1,), (1,)), ((), ())), preferred_element_type=jnp.float32
    )
    if source.dtype == jnp.float32:
        new_grad = (empty, empty)[1] + lax.dot_general(
            source,
            pieces[1].astype(jnp.float32),
            (((1,), (1,)), ((), ())),
            precision=highest_precision,
        )
    else:
        new_grad = lax.dot_general(
            source, pieces[1], (((1,), (1,)), ((), ())), preferred_element_type=jnp.float32
        )
    live_count = lengths[0]
    positions = lax.iota(jnp.int32, rows_here)
    weights = jnp.where(positions < live_count, 1.0, 0.0).astype(jnp.float32) / live_count.astype(
        jnp.float32
    )
    scaled = new_grad * weights[:, None]
    grad_row = lax.dot_general(
        scaled, new_act, (((0,), (0,)), ((), ())), precision=highest_precision
    )
    grad_row = grad_row.reshape(1, proj_size * proj_size).astype(jnp.bfloat16)
    valid_full = lax.all_gather(valid_rows, "dp", axis=1, tiled=True)[0]
    my_index = lax.axis_index("dp")
    scores = lax.dot_general(
        lax.all_gather(grad_row, "dp", axis=0, tiled=True),
        valid_full,
        (((1,), (1,)), ((), ())),
        preferred_element_type=jnp.float32,
    )
    owned = domains == my_index
    kept = scores * owned.astype(jnp.float32)[:, None]
    gram = lax.dot_general(kept, scores, (((0,), (0,)), ((), ())), precision=highest_precision)
    return gram[None, None]


def solution(mesh):
    placed = (
        P("pipe", "dp", None),
        P("pipe", "dp", None),
        P(None, "dp"),
        P(None, "dp"),
        P("pipe", "dp", None),
        P("dp"),
        P(),
    )
    return jax.shard_map(
        body, mesh=mesh, in_specs=placed, out_specs=P("pipe", "dp", None, None), check_vma=False
    )
```

profile of v0, /device:TPU:4, one launch (start us, length us, event | category | flops | bytes accessed | tf_op | source)
XLA Modules:
  0.0 522.5 jit_solution(17948236121018723122)
XLA Ops:
  6.5 0.0 copy-start
  6.5 0.0 all-gather.10.cloned.1.call-start
  6.5 0.7 all-gather.10.cloned.1.call-update
  7.3 0.0 all-gather.6.cloned.1.call-start
  7.3 0.7 all-gather.6.cloned.1.call-update
  8.0 0.0 all-gather.8.cloned.1.call-start
  8.1 0.7 all-gather.8.cloned.1.call-update
  8.7 0.0 all-gather.12.cloned.1.call-start
  8.8 1.4 copy.10
  10.1 0.0 all-gather.12.cloned.1.call-update
  10.9 0.7 compare_convert_fusion
  11.5 134.6 %all-gather.10.cloned.1.call-done = bf16[64,8192]{1,0:T(8,128)(2,1)} async-done(((bf16[64,128]{1,0:T(8,128)(2,1)}), bf16[64,8192]{1,0:T(8,128)(2,1)}) %all-gather.10.cloned.1.call-update) | async-done | bytes 1048592 | tf_op jit(solution)/shard_map/all_gather | solution.py:37
  146.1 0.0 copy-done
  146.1 2.1 fusion.2
  148.2 88.0 %all-gather.6.cloned.1.call-done = bf16[8,128,8192]{2,1,0:T(8,128)(2,1)} async-done(((bf16[1,128,8192]{2,1,0:T(8,128)(2,1)}), bf16[8,128,8192]{2,1,0:T(8,128)(2,1)}) %all-gather.6.cloned.1.call-update) | async-done | bytes 16777232 | tf_op jit(solution)/shard_map/all_gather | solution.py:11
  236.1 41.8 %while.16 = (s32[]{:T(128)}, f32[128,8192]{1,0:T(8,128)}, s32[]{:T(128)}, bf16[8,128,8192]{2,1,0:T(8,128)(2,1)}, s32[]{:T(128)}, /*index=5*/s32[]{:T(128)}, s32[]{:T(128)}, s32[]{:T(128)}) while((s32[]{:T(128)}, f32[128,8192]{1,0:T(8,128)}, s32[]{:T(128)}, bf16[8,128,8192]{2,1,0:T(8,128)(2,1)}, s32[]{:T(128)}, ...), condition=%wide.region_1.2_spmd.clone, body=%wide.region_0.1_spmd.clone.sunk | while | flops 4194312 | bytes 10485915 | solution.py:20
  236.1 4.1 add_select_fusion.2
  240.2 5.4 %add_select_fusion.2 = f32[128,8192]{1,0:T(8,128)} fusion(f32[128,8192]{1,0:T(8,128)} %get-tuple-element.173, bf16[8,128,8192]{2,1,0:T(8,128)(2,1)} %get-tuple-element.183, s32[]{:T(128)S(6)} %select_n.54, pred[]{:T(512)S(6)} %compare.3, pred[]{:T(512)S(6)} %gt.12), kind=kLoop, calls=%fused_computation.clone.1 | loop fusion | flops 4194304 | bytes 10485766 | tf_op jit(solution)/shard_map/while/body/eval_jaxpr/jit(_where)/select_n | solution.py:18
  245.6 5.4 %add_select_fusion.2 = f32[128,8192]{1,0:T(8,128)} fusion(f32[128,8192]{1,0:T(8,128)} %get-tuple-element.173, bf16[8,128,8192]{2,1,0:T(8,128)(2,1)} %get-tuple-element.183, s32[]{:T(128)S(6)} %select_n.54, pred[]{:T(512)S(6)} %compare.3, pred[]{:T(512)S(6)} %gt.12), kind=kLoop, calls=%fused_computation.clone.1 | loop fusion | flops 4194304 | bytes 10485766 | tf_op jit(solution)/shard_map/while/body/eval_jaxpr/jit(_where)/select_n | solution.py:18
  251.0 5.4 %add_select_fusion.2 = f32[128,8192]{1,0:T(8,128)} fusion(f32[128,8192]{1,0:T(8,128)} %get-tuple-element.173, bf16[8,128,8192]{2,1,0:T(8,128)(2,1)} %get-tuple-element.183, s32[]{:T(128)S(6)} %select_n.54, pred[]{:T(512)S(6)} %compare.3, pred[]{:T(512)S(6)} %gt.12), kind=kLoop, calls=%fused_computation.clone.1 | loop fusion | flops 4194304 | bytes 10485766 | tf_op jit(solution)/shard_map/while/body/eval_jaxpr/jit(_where)/select_n | solution.py:18
  256.4 5.4 %add_select_fusion.2 = f32[128,8192]{1,0:T(8,128)} fusion(f32[128,8192]{1,0:T(8,128)} %get-tuple-element.173, bf16[8,128,8192]{2,1,0:T(8,128)(2,1)} %get-tuple-element.183, s32[]{:T(128)S(6)} %select_n.54, pred[]{:T(512)S(6)} %compare.3, pred[]{:T(512)S(6)} %gt.12), kind=kLoop, calls=%fused_computation.clone.1 | loop fusion | flops 4194304 | bytes 10485766 | tf_op jit(solution)/shard_map/while/body/eval_jaxpr/jit(_where)/select_n | solution.py:18
  261.8 5.4 %add_select_fusion.2 = f32[128,8192]{1,0:T(8,128)} fusion(f32[128,8192]{1,0:T(8,128)} %get-tuple-element.173, bf16[8,128,8192]{2,1,0:T(8,128)(2,1)} %get-tuple-element.183, s32[]{:T(128)S(6)} %select_n.54, pred[]{:T(512)S(6)} %compare.3, pred[]{:T(512)S(6)} %gt.12), kind=kLoop, calls=%fused_computation.clone.1 | loop fusion | flops 4194304 | bytes 10485766 | tf_op jit(solution)/shard_map/while/body/eval_jaxpr/jit(_where)/select_n | solution.py:18
  267.1 5.4 %add_select_fusion.2 = f32[128,8192]{1,0:T(8,128)} fusion(f32[128,8192]{1,0:T(8,128)} %get-tuple-element.173, bf16[8,128,8192]{2,1,0:T(8,128)(2,1)} %get-tuple-element.183, s32[]{:T(128)S(6)} %select_n.54, pred[]{:T(512)S(6)} %compare.3, pred[]{:T(512)S(6)} %gt.12), kind=kLoop, calls=%fused_computation.clone.1 | loop fusion | flops 4194304 | bytes 10485766 | tf_op jit(solution)/shard_map/while/body/eval_jaxpr/jit(_where)/select_n | solution.py:18
  272.5 5.4 %add_select_fusion.2 = f32[128,8192]{1,0:T(8,128)} fusion(f32[128,8192]{1,0:T(8,128)} %get-tuple-element.173, bf16[8,128,8192]{2,1,0:T(8,128)(2,1)} %get-tuple-element.183, s32[]{:T(128)S(6)} %select_n.54, pred[]{:T(512)S(6)} %compare.3, pred[]{:T(512)S(6)} %gt.12), kind=kLoop, calls=%fused_computation.clone.1 | loop fusion | flops 4194304 | bytes 10485766 | tf_op jit(solution)/shard_map/while/body/eval_jaxpr/jit(_where)/select_n | solution.py:18
  277.9 93.9 %all-gather.8.cloned.1.call-done = bf16[64,8192]{1,0:T(8,128)(2,1)} async-done(((bf16[64,128]{1,0:T(8,128)(2,1)}), bf16[64,8192]{1,0:T(8,128)(2,1)}) %all-gather.8.cloned.1.call-update) | async-done | bytes 1048592 | tf_op jit(solution)/shard_map/all_gather | solution.py:38
  371.8 5.8 %fusion.4 = f32[128,64]{0,1:T(8,128)S(1)} fusion(bf16[64,8192]{1,0:T(8,128)(2,1)} %all-gather.8.cloned.1.call-done, f32[128,8192]{1,0:T(8,128)} %get-tuple-element.115, bf16[1,128,8192]{2,1,0:T(8,128)(2,1)} %param.10, f32[128]{0:T(128)S(1)} %fusion.12), kind=kOutput, calls=%fused_computation.7 | convolution fusion | flops 807411712 | bytes 7373312 | tf_op jit(solution)/shard_map/dot_general | solution.py:44
  377.6 0.2 convolution_convert_fusion
  377.8 0.1 reshape.28
  377.9 100.0 %all-gather = bf16[64,1,4096]{2,1,0:T(2,128)(2,1)S(1)} all-gather(bf16[1,1,4096]{2,1,0:T(2,128)(2,1)S(1)} %reshape.28), channel_id=1, replica_groups=mesh['pipe'=8,'dp'=64] {'dp'}, dimensions={0}, use_global_device_ids=true | all-gather | bytes 532480 | tf_op jit(solution)/shard_map/all_gather | solution.py:67
  477.8 33.8 %all-gather.12.cloned.1.call-done = bf16[1,128,4096]{2,0,1:T(2,128)(2,1)} async-done(((bf16[1,2,4096]{2,0,1:T(2,128)(2,1)}), bf16[1,128,4096]{2,0,1:T(2,128)(2,1)}) %all-gather.12.cloned.1.call-update) | async-done | bytes 1048592 | tf_op jit(solution)/shard_map/all_gather | solution.py:64
  511.7 3.3 fusion.5
  515.0 1.0 convolution_bitcast_fusion
  (2 shorter events, 0.0 us)
Async XLA Ops:
  6.5 139.6 %copy-start = (bf16[1,128,8192]{2,1,0:T(8,128)(2,1)S(1)}, bf16[1,128,8192]{2,1,0:T(8,128)(2,1)}, u32[]{:S(2)}) copy-start(bf16[1,128,8192]{2,1,0:T(8,128)(2,1)} %param.9) | copy-start | bytes 6291460
  6.5 139.6 %all-gather.10.cloned.1.call-start = ((), (), s32[]{:S(2)}) async-start(), calls=%async_computation.2 | async-start | bytes 1064960 | tf_op jit(solution)/shard_map/all_gather | solution.py:37
  7.3 228.9 %all-gather.6.cloned.1.call-start = ((), (), s32[]{:S(2)}) async-start(), calls=%async_computation | async-start | bytes 18874368 | tf_op jit(solution)/shard_map/all_gather | solution.py:11
  8.0 363.8 %all-gather.8.cloned.1.call-start = ((), (), s32[]{:S(2)}) async-start(), calls=%async_computation.1 | async-start | bytes 1064960 | tf_op jit(solution)/shard_map/all_gather | solution.py:38
  8.7 502.9 %all-gather.12.cloned.1.call-start = ((), (), s32[]{:S(2)}) async-start(), calls=%async_computation.3 | async-start | bytes 2129920 | tf_op jit(solution)/shard_map/all_gather | solution.py:64
Sparse Core Ops, SparseCore 0:
  10.3 135.7 all-gather.9
  148.3 87.8 all-gather.5
  239.1 132.7 all-gather.7
  374.6 137.0 all-gather.11
where the time goes:
time: 523 us
  waiting for transfers between devices  352 us (67%)
  blocking collectives  100 us (19%)
  other arithmetic  42.4 us (8%)
  between operations  13.8 us (3%)
  matrix products  12.3 us (2%)
    all_gather x1, waiting for transfers between devices, body(): lax.all_gather(proj_in, 'dp', axis=1, tiled=True)  135 us
    all_gather x1, blocking collectives, body(): lax.all_gather(grad_row, 'dp', axis=0, tiled=True)  100 us
    all_gather x1, waiting for transfers between devices, body(): lax.all_gather(proj_out, 'dp', axis=1, tiled=True)  93.9 us
    all_gather x1, waiting for transfers between devices, entering(): everything = lax.all_gather(value.astype(jnp.bfloat16), axis)  88 us
    select_n x8, other arithmetic, lap(): return jnp.where(reached, new, before)  41.8 us
    all_gather x1, waiting for transfers between devices, body(): valid_full = lax.all_gather(valid_rows, 'dp', axis=1, tiled=True)[0]  33.8 us
  transfers between devices with their start and end apart: 4, of which 4 were waited for; matrix products, arithmetic and copies ran while one was open for 10% of the time, Pallas kernels for 0%

commit v1 on v0

--- a/solution.py
+++ b/solution.py
@@ -64,7 +64,9 @@
     valid_full = lax.all_gather(valid_rows, "dp", axis=1, tiled=True)[0]
     my_index = lax.axis_index("dp")
     scores = lax.dot_general(
-        lax.all_gather(grad_row, "dp", axis=0, tiled=True),
+        jnp.concatenate(
+            lax.all_to_all(jnp.stack([grad_row] * lax.axis_size("dp")), "dp", 0, 0), axis=0
+        ),
         valid_full,
         (((1,), (1,)), ((), ())),
         preferred_element_type=jnp.float32,

time: 523 us -> 553 us (1.057)
  the two profiles are of different devices: /device:TPU:4 before, /device:TPU:2 now
where the time goes in v1:
time: 553 us
  waiting for transfers between devices  463 us (84%)
  other arithmetic  46.4 us (8%)
  between operations  13.9 us (3%)
  matrix products  12.7 us (2%)
  starting transfers between devices  10.3 us (2%)
  local copies, waits for them, and re-layouts  6.3 us (1%)
    all_gather x1, waiting for transfers between devices, body(): lax.all_gather(proj_in, 'dp', axis=1, tiled=True)  137 us
    all_gather x1, waiting for transfers between devices, body(): valid_full = lax.all_gather(valid_rows, 'dp', axis=1, tiled=True)[0]  122 us
    all_gather x1, waiting for transfers between devices, body(): lax.all_gather(proj_out, 'dp', axis=1, tiled=True)  93.5 us
    all_gather x1, waiting for transfers between devices, entering(): everything = lax.all_gather(value.astype(jnp.bfloat16), axis)  88.3 us
    select_n x8, other arithmetic, lap(): return jnp.where(reached, new, before)  41.8 us
    all_to_all x1, waiting for transfers between devices, body(): lax.all_to_all(jnp.stack([grad_row] * lax.axis_size('dp')), 'dp', 0, 0)  21.1 us
  transfers between devices with their start and end apart: 5, of which 5 were waited for; matrix products, arithmetic and copies ran while one was open for 8% of the time, Pallas kernels for 0%

profile of v1, /device:TPU:2, one launch (start us, length us, event | category | flops | bytes accessed | tf_op | source)
XLA Modules:
  0.0 552.9 jit_solution(13797642606581695799)
XLA Ops:
  6.5 0.0 copy-start
  6.5 0.0 all-gather.9.cloned.1.call-start
  6.5 0.7 all-gather.9.cloned.1.call-update
  7.3 0.0 all-gather.5.cloned.1.call-start
  7.3 0.7 all-gather.5.cloned.1.call-update
  8.0 0.0 all-gather.7.cloned.1.call-start
  8.1 0.7 all-gather.7.cloned.1.call-update
  9.4 136.7 %all-gather.9.cloned.1.call-done = bf16[64,8192]{1,0:T(8,128)(2,1)} async-done(((bf16[64,128]{1,0:T(8,128)(2,1)}), bf16[64,8192]{1,0:T(8,128)(2,1)}) %all-gather.9.cloned.1.call-update) | async-done | bytes 1048592 | tf_op jit(solution)/shard_map/all_gather | solution.py:37
  146.1 0.0 copy-done
  146.1 2.1 fusion.2
  148.2 88.3 %all-gather.5.cloned.1.call-done = bf16[8,128,8192]{2,1,0:T(8,128)(2,1)} async-done(((bf16[1,128,8192]{2,1,0:T(8,128)(2,1)}), bf16[8,128,8192]{2,1,0:T(8,128)(2,1)}) %all-gather.5.cloned.1.call-update) | async-done | bytes 16777232 | tf_op jit(solution)/shard_map/all_gather | solution.py:11
  236.5 41.8 %while.16 = (s32[]{:T(128)}, f32[128,8192]{1,0:T(8,128)}, s32[]{:T(128)}, bf16[8,128,8192]{2,1,0:T(8,128)(2,1)}, s32[]{:T(128)}, /*index=5*/s32[]{:T(128)}, s32[]{:T(128)}, s32[]{:T(128)}) while((s32[]{:T(128)}, f32[128,8192]{1,0:T(8,128)}, s32[]{:T(128)}, bf16[8,128,8192]{2,1,0:T(8,128)(2,1)}, s32[]{:T(128)}, ...), condition=%wide.region_1.2_spmd.clone, body=%wide.region_0.1_spmd.clone.sunk | while | flops 4194312 | bytes 10485915 | solution.py:20
  236.5 4.1 add_select_fusion.2
  240.6 5.4 add_select_fusion.2
  246.0 5.4 add_select_fusion.2
  251.3 5.4 add_select_fusion.2
  256.7 5.4 add_select_fusion.2
  262.1 5.4 add_select_fusion.2
  267.5 5.4 add_select_fusion.2
  272.9 5.4 add_select_fusion.2
  278.3 93.5 %all-gather.7.cloned.1.call-done = bf16[64,8192]{1,0:T(8,128)(2,1)} async-done(((bf16[64,128]{1,0:T(8,128)(2,1)}), bf16[64,8192]{1,0:T(8,128)(2,1)}) %all-gather.7.cloned.1.call-update) | async-done | bytes 1048592 | tf_op jit(solution)/shard_map/all_gather | solution.py:38
  371.8 5.8 %fusion.4 = f32[128,64]{0,1:T(8,128)S(1)} fusion(bf16[64,8192]{1,0:T(8,128)(2,1)} %all-gather.7.cloned.1.call-done, f32[128,8192]{1,0:T(8,128)} %get-tuple-element.115, bf16[1,128,8192]{2,1,0:T(8,128)(2,1)} %param.10, f32[128]{0:T(128)S(1)} %fusion.12), kind=kOutput, calls=%fused_computation.7 | convolution fusion | flops 807411712 | bytes 7373312 | tf_op jit(solution)/shard_map/dot_general | solution.py:44
  377.6 0.0 copy-start.1
  377.6 0.0 copy-start.2
  377.6 0.2 convolution_convert_fusion
  377.8 0.1 convert_element_type.44
  377.9 1.0 stack.2
  378.9 0.5 broadcast.25
  379.4 4.6 reduce
  384.0 2.2 reshape.32
  386.2 10.2 %all-to-all-start = ((bf16[64,2,2048]{2,1,0:T(2,128)(2,1)}), bf16[64,2,2048]{2,1,0:T(2,128)(2,1)S(1)}, u32[]{:S(2)}, u32[]{:S(2)}) async-start(bf16[64,2,2048]{2,1,0:T(2,128)(2,1)} %reshape.32), calls=%async_computation | async-start | bytes 1048576 | tf_op jit(solution)/shard_map/all_to_all | solution.py:68
  396.5 0.0 all-gather.11.cloned.1.call-start
  396.5 0.0 copy-done.1
  396.5 0.6 copy.9
  397.2 0.0 all-gather.11.cloned.1.call-update
  397.2 0.0 copy-done.2
  397.2 21.1 %all-to-all-done = bf16[64,2,2048]{2,1,0:T(2,128)(2,1)S(1)} async-done(((bf16[64,2,2048]{2,1,0:T(2,128)(2,1)}), bf16[64,2,2048]{2,1,0:T(2,128)(2,1)S(1)}, u32[]{:S(2)}, u32[]{:S(2)}) %all-to-all-start) | async-done | bytes 524320 | tf_op jit(solution)/shard_map/all_to_all | solution.py:68
  418.3 1.8 reshape.33
  420.1 121.6 %all-gather.11.cloned.1.call-done = bf16[1,128,4096]{2,0,1:T(2,128)(2,1)} async-done(((bf16[1,2,4096]{2,0,1:T(2,128)(2,1)}), bf16[1,128,4096]{2,0,1:T(2,128)(2,1)}) %all-gather.11.cloned.1.call-update) | async-done | bytes 1048592 | tf_op jit(solution)/shard_map/all_gather | solution.py:64
  541.8 3.6 fusion.5
  545.4 1.0 convolution_bitcast_fusion
  (3 shorter events, 0.0 us)
Async XLA Ops:
  6.5 139.6 %copy-start = (bf16[1,128,8192]{2,1,0:T(8,128)(2,1)S(1)}, bf16[1,128,8192]{2,1,0:T(8,128)(2,1)}, u32[]{:S(2)}) copy-start(bf16[1,128,8192]{2,1,0:T(8,128)(2,1)} %param.9) | copy-start | bytes 6291460
  6.5 139.6 %all-gather.9.cloned.1.call-start = ((), (), s32[]{:S(2)}) async-start(), calls=%async_computation.3 | async-start | bytes 1064960 | tf_op jit(solution)/shard_map/all_gather | solution.py:37
  7.3 229.2 %all-gather.5.cloned.1.call-start = ((), (), s32[]{:S(2)}) async-start(), calls=%async_computation.1 | async-start | bytes 18874368 | tf_op jit(solution)/shard_map/all_gather | solution.py:11
  8.0 363.8 %all-gather.7.cloned.1.call-start = ((), (), s32[]{:S(2)}) async-start(), calls=%async_computation.2 | async-start | bytes 1064960 | tf_op jit(solution)/shard_map/all_gather | solution.py:38
  377.6 18.9 %copy-start.1 = (bf16[1,2,4096]{2,1,0:T(2,128)(2,1)S(1)}, bf16[1,2,4096]{2,1,0:T(2,128)(2,1)}, u32[]{:S(2)}) copy-start(bf16[1,2,4096]{2,1,0:T(2,128)(2,1)} %param.13) | copy-start | bytes 49156
  377.6 19.6 %copy-start.2 = (s32[64]{0:T(128)S(1)}, s32[64]{0:T(128)}, u32[]{:S(2)}) copy-start(s32[64]{0:T(128)} %param.15) | copy-start | bytes 772
  386.2 32.1 %all-to-all-start = ((bf16[64,2,2048]{2,1,0:T(2,128)(2,1)}), bf16[64,2,2048]{2,1,0:T(2,128)(2,1)S(1)}, u32[]{:S(2)}, u32[]{:S(2)}) async-start(bf16[64,2,2048]{2,1,0:T(2,128)(2,1)} %reshape.32), calls=%async_computation | async-start | bytes 1048576 | tf_op jit(solution)/shard_map/all_to_all | solution.py:68
  396.5 145.3 %all-gather.11.cloned.1.call-start = ((), (), s32[]{:S(2)}) async-start(), calls=%async_computation.4 | async-start | bytes 2129920 | tf_op jit(solution)/shard_map/all_gather | solution.py:64
Sparse Core Ops, SparseCore 0:
  10.3 135.7 all-gather.8
  148.2 88.1 all-gather.4
  239.4 132.3 all-gather.6
  399.9 141.7 all-gather.10
